TPU v7x, 32 devices: a whole 2x2x4 slice. The times are simulated.
32 devices in a mesh: rhs: 16 (over z, x, core), fac: 2 (over y).
Axes of the slice: x: 2, y: 2, z: 4, core: 2. Of those that a mesh axis runs over, the one named last changes fastest.
Arguments:
- right_sides: bfloat16 [1024, 768], P('rhs', 'fac'), may hold values from -6 to 6
- stripe: bfloat16 [768, 768], P('fac', 'rhs'), may hold values from -0.109375 to 0.109375
- inverses: float32 [2, 384, 384], P('fac'), may hold values from -2 to 2, as said below
- structure: int32 [2, 2], replicated, may hold values 0 or 1
- heater_wattages: bfloat16 [256, 1024], P(None, 'rhs'), may hold values from -0.25 to 0.25
Outputs:
- unknown_vector_results: bfloat16 [1024, 768], P('rhs', 'fac')
- thermal_field_reply: float32 [256, 768], P('rhs', 'fac')
Inputs may be any that keep to these rules, and one draw needn't show every extreme that they name: Each inverses[s] is lower triangular with its diagonal between 0.5 and 2.
All inputs are finite; a program needn't handle non-finite values.
Results may differ from a plain program's by a relative error of at most 0.0095.
Values may be sent and summed in bfloat16 or wider, within the bound.
A program may use at most 64 MiB of HBM per device.

v0:
```python
import jax
import jax.numpy as jnp
from jax import lax
from jax.sharding import PartitionSpec as P


def against_rows(left, right):
    return lax.dot_general(
        left, right, (((1,), (1,)), ((), ())), preferred_element_type=jnp.float32
    )


def body(right_sides, stripe, inverses, structure, heater_wattages):
    block_width = inverses.shape[1]
    supers_count = lax.axis_size("fac")
    resident_position = lax.axis_index("fac")
    right_hand_count = right_sides.shape[0]
    total_rows = block_width * supers_count
    stripe_rows, all_sides = (
        lax.all_gather(stripe, "fac", axis=0, tiled=True),
        lax.all_gather(right_sides, "fac", axis=1, tiled=True),
    )
    every_block_inverse = lax.all_gather(inverses, "fac", axis=0, tiled=True)
    whole = lax.all_gather(stripe_rows, "rhs", axis=1, tiled=True)
    forward_sweep = jnp.zeros((right_hand_count, total_rows), jnp.bfloat16)
    for block in range(supers_count):
        low = block * block_width
        col_mask = jnp.repeat(structure[block], block_width).astype(jnp.bfloat16)
        update = against_rows(forward_sweep * col_mask, whole[low : low + block_width])
        remainder = all_sides[:, low : low + block_width].astype(jnp.float32) - update
        finished_unknowns = jnp.dot(
            remainder, every_block_inverse[block].T, precision=lax.Precision.HIGHEST
        )
        forward_sweep = forward_sweep.at[:, low : low + block_width].set(
            finished_unknowns.astype(jnp.bfloat16)
        )
    unknown_vector_results = jnp.zeros((right_hand_count, total_rows), jnp.bfloat16)
    for block in range(supers_count - 1, -1, -1):
        low = block * block_width
        row_mask = jnp.repeat(structure[:, block], block_width).astype(jnp.bfloat16)
        update = jnp.dot(
            unknown_vector_results * row_mask,
            whole[:, low : low + block_width],
            preferred_element_type=jnp.float32,
        )
        remainder = forward_sweep[:, low : low + block_width].astype(jnp.float32) - update
        finished_unknowns = jnp.dot(
            remainder, every_block_inverse[block], precision=lax.Precision.HIGHEST
        )
        unknown_vector_results = unknown_vector_results.at[:, low : low + block_width].set(
            finished_unknowns.astype(jnp.bfloat16)
        )
    resident_panel = lax.dynamic_slice_in_dim(
        unknown_vector_results, resident_position * block_width, block_width, 1
    )
    thermal_field_reply = lax.psum_scatter(
        jnp.dot(heater_wattages, resident_panel, preferred_element_type=jnp.float32),
        "rhs",
        scatter_dimension=0,
        tiled=True,
    )
    return (resident_panel, thermal_field_reply)


def solution(mesh):
    placed = (P("rhs", "fac"), P("fac", "rhs"), P("fac", None, None), P(), P(None, "rhs"))
    return jax.shard_map(
        body,
        mesh=mesh,
        in_specs=placed,
        out_specs=(P("rhs", "fac"), P("rhs", "fac")),
        check_vma=False,
    )
```

profile of v0, /device:TPU:0, one launch (start us, length us, event | category | flops | bytes accessed | tf_op | source)
XLA Modules:
  0.0 146.0 jit_solution(7706581156529776256)
XLA Ops:
  7.2 7.3 %all_gather.13 = bf16[768,48]{0,1:T(8,128)(2,1)} all-gather(bf16[384,48]{0,1:T(8,128)(2,1)} %param.14), channel_id=1, replica_groups=mesh['rhs'=16,'fac'=2] {'fac'}, dimensions={0}, use_global_device_ids=true | all-gather | bytes 110592 | tf_op jit(solution)/shard_map/all_gather | solution.py:20
  14.5 0.0 all-gather.5.cloned.1.call-start
  14.6 0.7 all-gather.5.cloned.1.call-update
  15.3 0.7 convert.6
  16.0 0.1 broadcast_in_dim.16
  16.1 0.1 broadcast_in_dim.17
  16.2 0.2 slice_reduce_fusion
  16.4 0.1 broadcast_in_dim.18
  16.5 0.1 broadcast_in_dim.19
  16.6 0.6 compare_reduce_fusion
  17.2 5.0 %all_gather.12 = bf16[64,768]{1,0:T(8,128)(2,1)S(1)} all-gather(bf16[64,384]{1,0:T(8,128)(2,1)} %param.13), channel_id=1, replica_groups=mesh['rhs'=16,'fac'=2] {'fac'}, dimensions={1}, use_global_device_ids=true | all-gather | bytes 147456 | tf_op jit(solution)/shard_map/all_gather | solution.py:21
  22.2 31.3 %all-gather.3.cloned.1.call-done = bf16[768,768]{0,1:T(8,128)(2,1)} async-done(((bf16[768,48]{0,1:T(8,128)(2,1)}), bf16[768,768]{0,1:T(8,128)(2,1)}) %all-gather.3.cloned.1.call-update) | async-done | bytes 1179664 | tf_op jit(solution)/shard_map/all_gather | solution.py:24
  53.4 1.4 convolution_subtract_fusion.3
  54.8 21.9 %all-gather.5.cloned.1.call-done = f32[2,384,384]{2,1,0:T(8,128)} async-done(((f32[1,384,384]{2,1,0:T(8,128)}), f32[2,384,384]{2,1,0:T(8,128)}) %all-gather.5.cloned.1.call-update) | async-done | bytes 1179664 | tf_op jit(solution)/shard_map/all_gather | solution.py:23
  76.7 2.5 %fusion.1 = bf16[64,384]{1,0:T(8,128)(2,1)S(1)} fusion(f32[64,384]{1,0:T(8,128)S(1)} %convolution_subtract_fusion.3, f32[2,384,384]{2,1,0:T(8,128)} %all-gather.5.cloned.1.call-done, pred[]{:T(512)} %compare_reduce_fusion), kind=kOutput, calls=%fused_computation.10 | convolution fusion | flops 113295360 | bytes 737792 | tf_op jit(solution)/shard_map/dot_general | solution.py:31
  79.3 0.2 convolution_subtract_fusion.2
  79.5 0.7 fusion
  80.3 0.3 convolution_subtract_fusion.1
  80.6 0.5 convolution_convert_fusion.1
  81.1 0.3 convolution_subtract_fusion
  81.4 1.1 fusion.2
  82.5 0.2 convolution_bitcast_fusion
  82.8 0.9 copy.9
  83.7 55.7 %reduce-scatter.4.cloned.1.call-done = f32[16,384]{1,0:T(8,128)} async-done(((f32[256,384]{1,0:T(8,128)}), f32[16,384]{1,0:T(8,128)}) %reduce-scatter.4.cloned.1.call-update) | async-done | bytes 24592
  (18 shorter events, 0.3 us)
Async XLA Ops:
  7.2 75.4 %copy-start = (bf16[256,64]{0,1:T(8,128)(2,1)S(1)}, bf16[256,64]{0,1:T(8,128)(2,1)}, u32[]{:S(2)}) copy-start(bf16[256,64]{0,1:T(8,128)(2,1)} %param.17) | copy-start | bytes 98308
  7.2 46.2 %all-gather.3.cloned.1.call-start = ((), (), s32[]{:S(2)}) async-start(), calls=%async_computation.1 | async-start | bytes 1253376 | tf_op jit(solution)/shard_map/all_gather | solution.py:24
  14.5 62.2 %all-gather.5.cloned.1.call-start = ((), (), s32[]{:S(2)}) async-start(), calls=%async_computation.2 | async-start | bytes 1769472 | tf_op jit(solution)/shard_map/all_gather | solution.py:23
  15.3 124.2 %reduce-scatter.4.cloned.1.call-start = ((), (), s32[]{:S(2)}) async-start(), calls=%async_computation.3 | async-start | bytes 417792
  53.4 25.9 %copy-start.2 = (bf16[768,768]{0,1:T(8,128)(2,1)S(1)}, bf16[768,768]{0,1:T(8,128)(2,1)}, u32[]{:S(2)}) copy-start(bf16[768,768]{0,1:T(8,128)(2,1)} %all-gather.3.cloned.1.call-done) | copy-start | bytes 3538948
  76.7 2.8 %copy-start.1 = (f32[2,384,384]{2,1,0:T(8,128)S(1)}, f32[2,384,384]{2,1,0:T(8,128)}, u32[]{:S(2)}) copy-start(f32[2,384,384]{2,1,0:T(8,128)} %all-gather.5.cloned.1.call-done) | copy-start | bytes 3538948
  82.5 56.9 %copy-start.3 = (bf16[64,384]{1,0:T(8,128)(2,1)}, bf16[64,384]{1,0:T(8,128)(2,1)S(1)}, u32[]{:S(2)}) copy-start(bf16[64,384]{1,0:T(8,128)(2,1)S(1)} %fusion.11) | copy-start | bytes 147460
Sparse Core Ops, SparseCore 0:
  14.6 38.7 all-gather.2
  55.0 21.7 all-gather.4
  83.9 55.5 reduce-scatter.3
where the time goes:
time: 146 us
  waiting for transfers between devices  110 us (75%)
  between operations  13.8 us (9%)
  blocking collectives  12.2 us (8%)
  matrix products  7.3 us (5%)
  other arithmetic  1.55 us (1%)
    unnamed x4, waiting for transfers between devices  56.4 us
    all_gather x1, waiting for transfers between devices, body(): whole = lax.all_gather(stripe_rows, 'rhs', axis=1, tiled=True)  31.3 us
    all_gather x1, waiting for transfers between devices, body(): every_block_inverse = lax.all_gather(inverses, 'fac', axis=0, tiled=True)  21.9 us
    all_gather x1, blocking collectives, body(): lax.all_gather(stripe, 'fac', axis=0, tiled=True)  7.25 us
    all_gather x1, blocking collectives, body(): lax.all_gather(right_sides, 'fac', axis=1, tiled=True)  4.97 us
    dot_general x2, matrix products, body(): jnp.dot(remainder, every_block_inverse[block].T, precision=lax.Precision....  3.28 us
  transfers between devices with their start and end apart: 3, of which 3 were waited for; matrix products, arithmetic and copies ran while one was open for 2% of the time, Pallas kernels for 0%

commit v1 on v0

v1 whole, which is shorter than its diff:
```python
import functools

import jax
import jax.numpy as jnp
from jax import lax
from jax.experimental import pallas as pl
from jax.experimental.pallas import tpu as pltpu
from jax.sharding import PartitionSpec as P

F32 = jnp.float32
BF16 = jnp.bfloat16
NT = (((1,), (1,)), ((), ()))
NN = (((1,), (0,)), ((), ()))


def mul(left, right, dims):
    return lax.dot_general(left, right, dims, preferred_element_type=F32)


def split(value):
    high = value.astype(BF16)
    return high, (value - high.astype(F32)).astype(BF16)


def kernel(
    shape, sides_ref, stripe_ref, inverse_ref, structure_ref, watts_ref, out_ref, reply_ref,
    factor, high, low, acc, fwd, fwd_in, upd_out, upd_in, part, pair_out, pair_in, mine,
    sum_out, sum_in, z_send, x_send, c_send, factor_recv, f_send, f_recv, u_send, u_recv,
    pair_send, pair_recv, s_send, s_recv,
):
    supers, ranks, zs, xs = shape
    groups = ranks // 2
    width = inverse_ref.shape[1]
    count = sides_ref.shape[0]
    per = width // factor.shape[1]
    s = lax.axis_index("fac")
    me = lax.axis_index("rhs")
    core = lax.rem(me, 2)
    chip = lax.div(me, 2)
    x = lax.rem(chip, xs)
    z = lax.div(chip, xs)

    def rank(zz, xx, cc):
        return (zz * xs + xx) * 2 + cc

    def needed(b):
        return b < s * per

    barrier = pltpu.get_barrier_semaphore()
    for k in range(1, ranks):
        pl.semaphore_signal(barrier, inc=1, device_id={"rhs": lax.rem(me + k, ranks)})
    for k in range(1, supers):
        pl.semaphore_signal(barrier, inc=1, device_id={"fac": lax.rem(s + k, supers)})

    columns = factor.shape[1]

    @pl.when(needed(me))
    def _():
        eye = (
            lax.broadcasted_iota(jnp.int32, (columns, columns), 0)
            == lax.broadcasted_iota(jnp.int32, (columns, columns), 1)
        ).astype(F32).astype(BF16)
        factor[me] = mul(eye, stripe_ref[...], NT).astype(BF16)

    h, l = split(inverse_ref[0])
    high[...] = h
    low[...] = l
    acc[...] = sides_ref[...].astype(F32)

    def times_inverse(dims):
        a_high, a_low = split(acc[...])
        both = mul(jnp.concatenate([a_high, a_low], axis=0), high[...], dims)
        return both[:count] + both[count:] + mul(a_high, low[...], dims)

    @pl.when(s == 0)
    def _():
        fwd[...] = times_inverse(NT).astype(BF16)

    pl.semaphore_wait(barrier, ranks - 1 + supers - 1)

    def factor_copy(b, send, where):
        return pltpu.make_async_remote_copy(
            src_ref=factor.at[b], dst_ref=factor.at[b], send_sem=send,
            recv_sem=factor_recv.at[b], device_id={"rhs": where},
        )

    def forward_copy(t, k, where):
        return pltpu.make_async_remote_copy(
            src_ref=fwd, dst_ref=fwd_in.at[t], send_sem=f_send.at[k],
            recv_sem=f_recv.at[t], device_id={"fac": where},
        )

    def update_copy(t, where):
        return pltpu.make_async_remote_copy(
            src_ref=upd_out.at[where], dst_ref=upd_in.at[t], send_sem=u_send.at[where],
            recv_sem=u_recv.at[t], device_id={"fac": where},
        )

    @pl.when(s == 0)
    def _():
        for k in range(1, supers):
            forward_copy(0, k, k).start()

    for k in range(1, zs):
        @pl.when(needed(me))
        def _():
            factor_copy(me, z_send.at[k], rank(lax.rem(z + k, zs), x, core)).start()
    for k in range(zs):
        zz = lax.rem(z + zs - k, zs)
        b = rank(zz, x, core)

        @pl.when(needed(b))
        def _():
            if k > 0:
                factor_copy(b, z_send.at[0], me).wait_recv()
            for j in range(1, xs):
                factor_copy(b, x_send.at[k, j], rank(z, lax.rem(x + j, xs), core)).start()
            factor_copy(b, c_send.at[k, 0], rank(z, x, 1 - core)).start()
    for k in range(zs):
        zz = lax.rem(z + zs - k, zs)
        for j in range(1, xs):
            b = rank(zz, lax.rem(x + xs - j, xs), core)

            @pl.when(needed(b))
            def _():
                factor_copy(b, z_send.at[0], me).wait_recv()
                factor_copy(b, c_send.at[k, j], rank(z, x, 1 - core)).start()
    for zz in range(zs):
        for xx in range(xs):
            b = rank(zz, xx, 1 - core)

            @pl.when(needed(b))
            def _():
                factor_copy(b, z_send.at[0], me).wait_recv()

    def block(t):
        return factor[t * per:(t + 1) * per].reshape(width, width)

    for t in range(supers - 1):
        @pl.when(s > t)
        def _():
            forward_copy(t, 0, s).wait_recv()
            keep = structure_ref[s, t].astype(F32)
            acc[...] -= keep * mul(fwd_in[t], block(t), NN)

    @pl.when(s > 0)
    def _():
        fwd[...] = times_inverse(NT).astype(BF16)

    for k in range(2, supers):
        @pl.when((s > 0) & (s < k))
        def _():
            forward_copy(s, k, k).start()

    acc[...] = fwd[...].astype(F32)
    for t in range(supers - 1, 0, -1):
        @pl.when(s < t)
        def _():
            update_copy(t, s).wait_recv()
            acc[...] -= upd_in[t].astype(F32)
    solved = times_inverse(NN).astype(BF16)
    out_ref[...] = solved
    for t in range(supers - 2, -1, -1):
        @pl.when(s > t)
        def _():
            keep = structure_ref[s, t].astype(F32)
            upd_out[t] = (keep * mul(out_ref[...], block(t), NT)).astype(BF16)
            update_copy(s, t).start()

    part[...] = mul(watts_ref[...], out_ref[...], NN).reshape(part.shape)
    for g in range(groups):
        pair_out[g] = part[2 * g + 1 - core].astype(pair_out.dtype)
    pair = pltpu.make_async_remote_copy(
        src_ref=pair_out, dst_ref=pair_in, send_sem=pair_send, recv_sem=pair_recv,
        device_id={"rhs": rank(z, x, 1 - core)},
    )
    pair.start()
    pair.wait_recv()
    for g in range(groups):
        both = part[2 * g + core] + pair_in[g].astype(F32)
        mine[g] = both
        sum_out[g] = both.astype(sum_out.dtype)

    def sum_copy(target, source, k):
        return pltpu.make_async_remote_copy(
            src_ref=sum_out.at[target], dst_ref=sum_in.at[source], send_sem=s_send.at[k],
            recv_sem=s_recv.at[source], device_id={"rhs": target * 2 + core},
        )

    for k in range(1, groups):
        sum_copy(lax.rem(chip + k, groups), chip, k).start()
    total = mine[chip]
    for k in range(1, groups):
        source = lax.rem(chip + groups - k, groups)
        sum_copy(chip, source, 0).wait_recv()
        total = total + sum_in[source].astype(F32)
    reply_ref[...] = total

    for k in range(1, groups):
        sum_copy(lax.rem(chip + k, groups), chip, k).wait_send()
    pair.wait_send()
    for t in range(supers - 1):
        @pl.when(s > t)
        def _():
            update_copy(s, t).wait_send()
    for k in range(1, supers):
        @pl.when(s < k)
        def _():
            forward_copy(s, k, k).wait_send()
    for k in range(1, zs):
        @pl.when(needed(me))
        def _():
            factor_copy(me, z_send.at[k], me).wait_send()
    for k in range(zs):
        zz = lax.rem(z + zs - k, zs)
        for j in range(xs):
            b = rank(zz, lax.rem(x + xs - j, xs), core)

            @pl.when(needed(b))
            def _():
                factor_copy(b, c_send.at[k, j], me).wait_send()
            if j > 0:
                own = rank(zz, x, core)

                @pl.when(needed(own))
                def _():
                    factor_copy(own, x_send.at[k, j], me).wait_send()


def body(right_sides, stripe, inverses, structure, heater_wattages):
    supers = lax.axis_size("fac")
    ranks = lax.axis_size("rhs")
    zs = 4
    xs = ranks // (2 * zs)
    count, width = right_sides.shape
    columns = stripe.shape[1]
    loads = heater_wattages.shape[0]
    rows = loads // ranks
    groups = ranks // 2
    wire = BF16 if rows % 16 == 0 else F32
    dma = pltpu.SemaphoreType.DMA
    vmem = pl.BlockSpec(memory_space=pltpu.VMEM)
    return pl.pallas_call(
        functools.partial(kernel, (supers, ranks, zs, xs)),
        out_shape=(
            jax.ShapeDtypeStruct((count, width), BF16),
            jax.ShapeDtypeStruct((rows, width), F32),
        ),
        in_specs=[vmem, vmem, vmem, pl.BlockSpec(memory_space=pltpu.SMEM), vmem],
        out_specs=(vmem, vmem),
        scratch_shapes=[
            pltpu.VMEM((ranks, columns, width), BF16),
            pltpu.VMEM((width, width), BF16),
            pltpu.VMEM((width, width), BF16),
            pltpu.VMEM((count, width), F32),
            pltpu.VMEM((count, width), BF16),
            pltpu.VMEM((supers, count, width), BF16),
            pltpu.VMEM((supers, count, width), BF16),
            pltpu.VMEM((supers, count, width), BF16),
            pltpu.VMEM((ranks, rows, width), F32),
            pltpu.VMEM((groups, rows, width), wire),
            pltpu.VMEM((groups, rows, width), wire),
            pltpu.VMEM((groups, rows, width), F32),
            pltpu.VMEM((groups, rows, width), wire),
            pltpu.VMEM((groups, rows, width), wire),
            dma((zs,)), dma((zs, xs)), dma((zs, xs)), dma((ranks,)),
            dma((supers,)), dma((supers,)), dma((supers,)), dma((supers,)),
            dma, dma, dma((groups,)), dma((groups,)),
        ],
        compiler_params=pltpu.CompilerParams(
            collective_id=0, has_side_effects=True, vmem_limit_bytes=32 * 1024 * 1024
        ),
    )(right_sides, stripe, inverses, structure, heater_wattages)


def solution(mesh):
    placed = (P("rhs", "fac"), P("fac", "rhs"), P("fac", None, None), P(), P(None, "rhs"))
    return jax.shard_map(
        body,
        mesh=mesh,
        in_specs=placed,
        out_specs=(P("rhs", "fac"), P("rhs", "fac")),
        check_vma=False,
    )
```

time: 146 us -> 30.6 us (0.21)
  waiting for transfers between devices: 110 us -> 0 us
  Pallas kernels: 0 us -> 25.6 us
  between operations: 13.8 us -> 0.68 us
  blocking collectives: 12.2 us -> 0 us
  matrix products: 7.3 us -> 0 us
  local copies, waits for them, and re-layouts: 1.33 us -> 3.96 us
  other arithmetic: 1.55 us -> 0 us
    unnamed x4 -> x0, waiting for transfers between devices: 56.4 us -> none
    all_gather x2 -> x0, waiting for transfers between devices: 53.2 us -> none  [the longest x1 31.3 us: body(): whole = lax.all_gather(stripe_rows, 'rhs', axis=1, tiled=True)]
    pallas_call x0 -> x1, Pallas kernels: none -> 25.6 us  [body(): pl.pallas_call(functools.partial(kernel, (supers, ranks, zs, xs)), out_sh...]
    all_gather x2 -> x0, blocking collectives: 12.2 us -> none  [the longest x1 7.25 us: body(): lax.all_gather(stripe, 'fac', axis=0, tiled=True)]
    dot_general x9 -> x0, matrix products: 7.3 us -> none  [the longest x2 3.28 us: body(): jnp.dot(remainder, every_block_inverse[block].T, precision=lax.Precision....]
    unnamed x9 -> x12, local copies, waits for them, and re-layouts: 0.95 us -> 3.96 us
  transfers between devices with their start and end apart: 3 -> 0, of which waited for: 3 -> 0; matrix products, arithmetic and copies ran while one was open for 2% -> 0% of each run, Pallas kernels for 0% -> 0%
where the time goes in v1:
time: 30.6 us; the launch traced here: 30.3 us
  Pallas kernels  25.6 us (84%)
  local copies, waits for them, and re-layouts  3.96 us (13%)
  between operations  0.68 us (2%)
    pallas_call x1, Pallas kernels, body(): pl.pallas_call(functools.partial(kernel, (supers, ranks, zs, xs)), out_sh...  25.6 us
    unnamed x12, local copies, waits for them, and re-layouts  3.96 us

profile of v1, /device:TPU:0, one launch (start us, length us, event | category | flops | bytes accessed | tf_op | source)
XLA Modules:
  0.0 30.3 jit_solution(17902160843300533260)
XLA Ops:
  0.6 0.0 copy-start.3
  0.6 0.9 %copy.8.watts_ref = bf16[256,64]{1,0:T(8,128)(2,1)S(1)} copy(bf16[256,64]{0,1:T(8,128)(2,1)} %param.9) | data formatting | bytes 65536 | tf_op args[4]
  1.5 0.0 copy-done.3
  1.5 0.0 copy-start.1
  1.5 0.0 copy-start.2
  1.6 0.1 copy.7.stripe_ref
  1.7 0.7 %copy-done.1 = bf16[64,384]{1,0:T(8,128)(2,1)S(1)} copy-done((bf16[64,384]{1,0:T(8,128)(2,1)S(1)}, bf16[64,384]{1,0:T(8,128)(2,1)}, u32[]{:S(2)}) %copy-start.1) | copy-done | bytes 49176
  2.3 0.0 copy-done.2
  2.3 0.0 copy-start
  2.3 1.1 %copy-done = f32[1,384,384]{2,1,0:T(8,128)S(1)} copy-done((f32[1,384,384]{2,1,0:T(8,128)S(1)}, f32[1,384,384]{2,1,0:T(8,128)}, u32[]{:S(2)}) %copy-start) | copy-done | bytes 589848
  3.4 25.6 %shard_map.68 = (bf16[64,384]{1,0:T(8,128)(2,1)S(1)}, f32[16,384]{1,0:T(8,128)S(1)}) custom-call(bf16[64,384]{1,0:T(8,128)(2,1)S(1)} %copy-done.1, bf16[384,48]{1,0:T(8,128)(2,1)S(1)} %copy.7.stripe_ref, f32[1,384,384]{2,1,0:T(8,128)S(1)} %copy-done, s32[2,2]{1,0:T(2,128)S(1)} %copy-done.2, bf16[256,64]{1,0:T(8,128)(2,1)S(1)} %copy.8.watts_ref), custom_call_target="tpu_custom_call" | custom-call | tf_op jit(solution)/shard_map/pallas_call | solution.py:243
  29.0 0.6 %copy.11 = bf16[64,384]{1,0:T(8,128)(2,1)} copy(bf16[64,384]{1,0:T(8,128)(2,1)S(1)} %get-tuple-element.4) | data formatting | bytes 98304
  29.7 0.6 %copy.12 = f32[16,384]{1,0:T(8,128)} copy(f32[16,384]{1,0:T(8,128)S(1)} %get-tuple-element.5) | data formatting | bytes 49152
Async XLA Ops:
  0.6 0.9 %copy-start.3 = (bf16[384,48]{0,1:T(8,128)(2,1)S(1)}, bf16[384,48]{0,1:T(8,128)(2,1)}, u32[]{:S(2)}) copy-start(bf16[384,48]{0,1:T(8,128)(2,1)} %param.6) | copy-start | bytes 110596
  1.5 0.8 %copy-start.1 = (bf16[64,384]{1,0:T(8,128)(2,1)S(1)}, bf16[64,384]{1,0:T(8,128)(2,1)}, u32[]{:S(2)}) copy-start(bf16[64,384]{1,0:T(8,128)(2,1)} %sides_ref.1) | copy-start | bytes 147460
  1.5 0.8 %copy-start.2 = (s32[2,2]{1,0:T(2,128)S(1)}, s32[2,2]{1,0:T(2,128)}, u32[]{:S(2)}) copy-start(s32[2,2]{1,0:T(2,128)} %structure_ref.1) | copy-start | bytes 52
  2.3 1.1 %copy-start = (f32[1,384,384]{2,1,0:T(8,128)S(1)}, f32[1,384,384]{2,1,0:T(8,128)}, u32[]{:S(2)}) copy-start(f32[1,384,384]{2,1,0:T(8,128)} %inverse_ref.1) | copy-start | bytes 1769476

commit v2 on v1

v2 whole, which is shorter than its diff:
```python
import functools

import jax
import jax.numpy as jnp
from jax import lax
from jax.experimental import pallas as pl
from jax.experimental.pallas import tpu as pltpu
from jax.sharding import PartitionSpec as P

F32 = jnp.float32
BF16 = jnp.bfloat16
LIMIT = 64 * 1024 * 1024 - 160 * 1024
NT = (((1,), (1,)), ((), ()))
NN = (((1,), (0,)), ((), ()))


def mul(left, right, dims):
    return lax.dot_general(left, right, dims, preferred_element_type=F32)


def split(value):
    high = value.astype(BF16)
    return high, (value - high.astype(F32)).astype(BF16)


def kernel(
    shape, sides_any, stripe_any, inverse_any, structure_any, watts_any, out_any, reply_ref,
    out_ref, factor, sides, inverse, keeps, watts_in, watts, watts_own, plain, turned, base, fwd, fwd_in,
    upd_out, upd_in, pair_out, pair_in, mine, sum_out, sum_in,
    load, z_send, x_send, c_send, factor_recv, f_send, f_recv, u_send, u_recv,
    pair_send, pair_recv, s_send, s_recv,
):
    supers, ranks, zs, xs = shape
    groups = ranks // 2
    width = inverse.shape[0]
    per = width // factor.shape[1]
    s = lax.axis_index("fac")
    me = lax.axis_index("rhs")
    core = lax.rem(me, 2)
    chip = lax.div(me, 2)
    x = lax.rem(chip, xs)
    z = lax.div(chip, xs)

    def rank(zz, xx, cc):
        return (zz * xs + xx) * 2 + cc

    def needed(b):
        return b < s * per

    loads = [
        pltpu.make_async_copy(stripe_any, factor.at[me], load.at[0]),
        pltpu.make_async_copy(inverse_any.at[0], inverse, load.at[1]),
        pltpu.make_async_copy(sides_any, sides, load.at[2]),
        pltpu.make_async_copy(watts_any, watts_in, load.at[3]),
        pltpu.make_async_copy(structure_any, keeps, load.at[4]),
    ]
    for copy in loads:
        copy.start()

    barrier = pltpu.get_barrier_semaphore()
    pl.semaphore_signal(barrier, inc=1, device_id={"rhs": chip * 2 + 1 - core})
    for k in range(1, supers):
        pl.semaphore_signal(barrier, inc=1, device_id={"fac": lax.rem(s + k, supers)})
    for k in range(1, groups):
        pl.semaphore_signal(barrier, inc=1, device_id={"rhs": lax.rem(chip + k, groups) * 2 + core})
    loads[0].wait()
    pl.semaphore_wait(barrier, groups + supers - 1)

    def factor_copy(b, send, where):
        return pltpu.make_async_remote_copy(
            src_ref=factor.at[b], dst_ref=factor.at[b], send_sem=send,
            recv_sem=factor_recv.at[b], device_id={"rhs": where},
        )

    def forward_copy(t, k, where):
        return pltpu.make_async_remote_copy(
            src_ref=fwd, dst_ref=fwd_in.at[t], send_sem=f_send.at[k],
            recv_sem=f_recv.at[t], device_id={"fac": where},
        )

    def update_copy(t, where):
        return pltpu.make_async_remote_copy(
            src_ref=upd_out.at[where], dst_ref=upd_in.at[t], send_sem=u_send.at[where],
            recv_sem=u_recv.at[t], device_id={"fac": where},
        )

    @pl.when(needed(me))
    def _():
        for k in range(1, zs):
            factor_copy(me, z_send.at[k], rank(lax.rem(z + k, zs), x, core)).start()

    def relay(k):
        b = rank(lax.rem(z + zs - k, zs), x, core)

        @pl.when(needed(b))
        def _():
            if k > 0:
                factor_copy(b, z_send.at[0], me).wait_recv()
            for j in range(1, xs):
                factor_copy(b, x_send.at[k, j], rank(z, lax.rem(x + j, xs), core)).start()
            factor_copy(b, c_send.at[k, 0], rank(z, x, 1 - core)).start()

    relay(0)

    loads[1].wait()
    high, low = split(inverse[...])
    plain[:width] = high
    plain[width:] = low
    turned[:, :width] = high
    turned[:, width:2 * width] = low
    turned[:, 2 * width:] = high
    loads[2].wait()
    loads[4].wait()

    def twice(value):
        return jnp.concatenate([value, value], axis=1)

    def thrice(value):
        a_high, a_low = split(value)
        return jnp.concatenate([a_high, a_high, a_low], axis=1)

    @pl.when(s == 0)
    def _():
        fwd[...] = mul(twice(sides[...]), turned[:, :2 * width], NT).astype(BF16)
        for k in range(1, supers):
            forward_copy(0, k, k).start()

    for k in range(1, zs):
        relay(k)
    for k in range(zs):
        for j in range(1, xs):
            b = rank(lax.rem(z + zs - k, zs), lax.rem(x + xs - j, xs), core)

            @pl.when(needed(b))
            def _():
                factor_copy(b, z_send.at[0], me).wait_recv()
                factor_copy(b, c_send.at[k, j], rank(z, x, 1 - core)).start()

    loads[3].wait()
    watts[...] = watts_in[...].astype(F32).T.reshape(watts.shape)
    for g in range(groups):
        watts_own[g] = watts[2 * g + 1 - core]
        watts_own[groups + g] = watts[2 * g + core]

    for zz in range(zs):
        for xx in range(xs):
            b = rank(zz, xx, 1 - core)

            @pl.when(needed(b))
            def _():
                factor_copy(b, z_send.at[0], me).wait_recv()

    def block(t):
        return factor[t * per:(t + 1) * per].reshape(width, width)

    @pl.when(s > 0)
    def _():
        base[...] = sides[...].astype(F32)
        for t in range(supers - 1):
            @pl.when(s > t)
            def _():
                forward_copy(t, 0, s).wait_recv()
                keep = keeps[s, t].astype(F32)
                base[...] -= keep * mul(fwd_in[t], block(t), NN)
        fwd[...] = mul(thrice(base[...]), turned[...], NT).astype(BF16)
        for k in range(2, supers):
            @pl.when(s < k)
            def _():
                forward_copy(s, k, k).start()

    base[...] = mul(twice(fwd[...]), plain[...], NN)
    out_ref[...] = base[...].astype(BF16)
    for t in range(supers - 1, 0, -1):
        @pl.when(s < t)
        def _():
            update_copy(t, s).wait_recv()
            base[...] -= mul(twice(upd_in[t]), plain[...], NN)
            if t - 1 == 0:
                out_ref[...] = base[...].astype(BF16)
            else:
                @pl.when(s == t - 1)
                def _():
                    out_ref[...] = base[...].astype(BF16)
    for t in range(supers - 2, -1, -1):
        @pl.when(s > t)
        def _():
            keep = keeps[s, t].astype(F32)
            upd_out[t] = (keep * mul(out_ref[...], block(t), NT)).astype(BF16)
            update_copy(s, t).start()

    def product(first):
        rows = watts_own[first:first + groups]
        rows = rows.reshape(groups * rows.shape[1], rows.shape[2]).astype(BF16)
        return mul(rows, out_ref[...], NN).reshape(mine.shape)

    pair_out[...] = product(0).astype(pair_out.dtype)
    pair = pltpu.make_async_remote_copy(
        src_ref=pair_out, dst_ref=pair_in, send_sem=pair_send, recv_sem=pair_recv,
        device_id={"rhs": rank(z, x, 1 - core)},
    )
    pair.start()
    keep_out = pltpu.make_async_copy(out_ref, out_any, load.at[5])
    keep_out.start()
    mine[...] = product(groups)
    pair.wait_recv()
    both = mine[...] + pair_in[...].astype(F32)
    mine[...] = both
    sum_out[...] = both.astype(sum_out.dtype)

    def sum_copy(target, source, k):
        return pltpu.make_async_remote_copy(
            src_ref=sum_out.at[target], dst_ref=sum_in.at[source], send_sem=s_send.at[k],
            recv_sem=s_recv.at[source], device_id={"rhs": target * 2 + core},
        )

    for k in range(1, groups):
        sum_copy(lax.rem(chip + k, groups), chip, k).start()
    total = mine[chip]
    for k in range(1, groups):
        source = lax.rem(chip + groups - k, groups)
        sum_copy(chip, source, 0).wait_recv()
        total = total + sum_in[source].astype(F32)
    reply_ref[...] = total

    for k in range(1, groups):
        sum_copy(lax.rem(chip + k, groups), chip, k).wait_send()
    pair.wait_send()
    keep_out.wait()
    for t in range(supers - 1):
        @pl.when(s > t)
        def _():
            update_copy(s, t).wait_send()
    for k in range(1, supers):
        @pl.when(s < k)
        def _():
            forward_copy(s, k, k).wait_send()

    @pl.when(needed(me))
    def _():
        for k in range(1, zs):
            factor_copy(me, z_send.at[k], me).wait_send()
    for k in range(zs):
        own = rank(lax.rem(z + zs - k, zs), x, core)

        @pl.when(needed(own))
        def _():
            factor_copy(own, c_send.at[k, 0], me).wait_send()
            for j in range(1, xs):
                factor_copy(own, x_send.at[k, j], me).wait_send()
        for j in range(1, xs):
            b = rank(lax.rem(z + zs - k, zs), lax.rem(x + xs - j, xs), core)

            @pl.when(needed(b))
            def _():
                factor_copy(b, c_send.at[k, j], me).wait_send()


def write_out(solved_ref, reply_ref, solved_out, reply_out, sem):
    first = pltpu.make_async_copy(solved_ref, solved_out, sem.at[0])
    second = pltpu.make_async_copy(reply_ref, reply_out, sem.at[1])
    first.start()
    second.start()
    first.wait()
    second.wait()


def body(right_sides, stripe, inverses, structure, heater_wattages):
    supers = lax.axis_size("fac")
    ranks = lax.axis_size("rhs")
    zs = 4
    xs = ranks // (2 * zs)
    count, width = right_sides.shape
    columns = stripe.shape[1]
    loads = heater_wattages.shape[0]
    rows = loads // ranks
    groups = ranks // 2
    wire = BF16 if rows % 16 == 0 else F32
    dma = pltpu.SemaphoreType.DMA
    vmem = pl.BlockSpec(memory_space=pltpu.VMEM)
    whole = pl.BlockSpec(memory_space=pl.ANY)
    solved, reply = pl.pallas_call(
        functools.partial(kernel, (supers, ranks, zs, xs)),
        out_shape=(
            jax.ShapeDtypeStruct((count, width), BF16),
            jax.ShapeDtypeStruct((rows, width), F32),
        ),
        in_specs=[whole] * 5,
        out_specs=(whole, vmem),
        scratch_shapes=[
            pltpu.VMEM((count, width), BF16),
            pltpu.VMEM((ranks, columns, width), BF16),
            pltpu.VMEM((count, width), BF16),
            pltpu.VMEM((width, width), F32),
            pltpu.SMEM((supers, supers), jnp.int32),
            pltpu.VMEM((count, loads), BF16),
            pltpu.VMEM((ranks, rows, count), F32),
            pltpu.VMEM((ranks, rows, count), F32),
            pltpu.VMEM((2 * width, width), BF16),
            pltpu.VMEM((width, 3 * width), BF16),
            pltpu.VMEM((count, width), F32),
            pltpu.VMEM((count, width), BF16),
            pltpu.VMEM((supers, count, width), BF16),
            pltpu.VMEM((supers, count, width), BF16),
            pltpu.VMEM((supers, count, width), BF16),
            pltpu.VMEM((groups, rows, width), wire),
            pltpu.VMEM((groups, rows, width), wire),
            pltpu.VMEM((groups, rows, width), F32),
            pltpu.VMEM((groups, rows, width), wire),
            pltpu.VMEM((groups, rows, width), wire),
            dma((6,)), dma((zs,)), dma((zs, xs)), dma((zs, xs)), dma((ranks,)),
            dma((supers,)), dma((supers,)), dma((supers,)), dma((supers,)),
            dma, dma, dma((groups,)), dma((groups,)),
        ],
        compiler_params=pltpu.CompilerParams(
            collective_id=0, has_side_effects=True, vmem_limit_bytes=LIMIT
        ),
    )(right_sides, stripe.T, inverses, structure, heater_wattages.T)
    return pl.pallas_call(
        write_out,
        out_shape=(
            jax.ShapeDtypeStruct((count, width), BF16),
            jax.ShapeDtypeStruct((rows, width), F32),
        ),
        in_specs=[whole, whole],
        out_specs=(whole, whole),
        scratch_shapes=[dma((2,))],
    )(solved, reply)


def solution(mesh):
    placed = (P("rhs", "fac"), P("fac", "rhs"), P("fac", None, None), P(), P(None, "rhs"))
    return jax.shard_map(
        body,
        mesh=mesh,
        in_specs=placed,
        out_specs=(P("rhs", "fac"), P("rhs", "fac")),
        check_vma=False,
    )
```

time: 30.6 us -> 30.1 us (0.984)
  local copies, waits for them, and re-layouts: 3.96 us -> 0 us
  Pallas kernels: 25.6 us -> 29.3 us
    unnamed x12 -> x0, local copies, waits for them, and re-layouts: 3.96 us -> none
    pallas_call x0 -> x1, Pallas kernels: none -> 3.35 us  [body(): pl.pallas_call(write_out, out_shape=(jax.ShapeDtypeStruct((count, width),...]
    pallas_call x1, Pallas kernels: 25.6 us -> 26 us  [body(): pl.pallas_call(functools.partial(kernel, (supers, ranks, zs, xs)), out_sh...]
where the time goes in v2:
time: 30.1 us; the launch traced here: 30 us
  Pallas kernels  29.3 us (97%)
  between operations  0.64 us (2%)
    pallas_call x1, Pallas kernels, body(): pl.pallas_call(functools.partial(kernel, (supers, ranks, zs, xs)), out_sh...  26 us
    pallas_call x1, Pallas kernels, body(): pl.pallas_call(write_out, out_shape=(jax.ShapeDtypeStruct((count, width),...  3.35 us

profile of v2, /device:TPU:0, one launch (start us, length us, event | category | flops | bytes accessed | tf_op | source)
XLA Modules:
  0.0 30.0 jit_solution(15304253898970141564)
XLA Ops:
  0.6 26.0 %shard_map.68 = (bf16[64,384]{1,0:T(8,128)(2,1)}, f32[16,384]{1,0:T(8,128)}) custom-call(bf16[64,384]{1,0:T(8,128)(2,1)} %sides_any.1, bf16[48,384]{1,0:T(8,128)(2,1)} %bitcast.2, f32[1,384,384]{2,1,0:T(8,128)} %inverse_any.1, s32[2,2]{1,0:T(2,128)} %structure_any.1, bf16[64,256]{1,0:T(8,128)(2,1)} %bitcast.3), custom_call_target="tpu_custom_call" | custom-call | tf_op jit(solution)/shard_map/pallas_call | solution.py:281
  26.6 3.4 %shard_map.69 = (bf16[64,384]{1,0:T(8,128)(2,1)}, f32[16,384]{1,0:T(8,128)}) custom-call(bf16[64,384]{1,0:T(8,128)(2,1)} %get-tuple-element.4.solved_ref, f32[16,384]{1,0:T(8,128)} %get-tuple-element.5.reply_ref), custom_call_target="tpu_custom_call" | custom-call | tf_op jit(solution)/shard_map/pallas_call | solution.py:318

commit v3 on v2

--- a/solution.py
+++ b/solution.py
@@ -9,7 +9,7 @@
 
 F32 = jnp.float32
 BF16 = jnp.bfloat16
-LIMIT = 64 * 1024 * 1024 - 160 * 1024
+LIMIT = 32 * 1024 * 1024
 NT = (((1,), (1,)), ((), ()))
 NN = (((1,), (0,)), ((), ()))
 
@@ -24,8 +24,8 @@
 
 
 def kernel(
-    shape, sides_any, stripe_any, inverse_any, structure_any, watts_any, out_any, reply_ref,
-    out_ref, factor, sides, inverse, keeps, watts_in, watts, watts_own, plain, turned, base, fwd, fwd_in,
+    shape, sides_any, stripe_any, inverse_any, structure_any, watts_any, out_ref, reply_ref,
+    factor, sides, inverse, keeps, watts_in, watts, watts_own, plain, turned, base, fwd, fwd_in,
     upd_out, upd_in, pair_out, pair_in, mine, sum_out, sum_in,
     load, z_send, x_send, c_send, factor_recv, f_send, f_recv, u_send, u_recv,
     pair_send, pair_recv, s_send, s_recv,
@@ -199,8 +199,6 @@
         device_id={"rhs": rank(z, x, 1 - core)},
     )
     pair.start()
-    keep_out = pltpu.make_async_copy(out_ref, out_any, load.at[5])
-    keep_out.start()
     mine[...] = product(groups)
     pair.wait_recv()
     both = mine[...] + pair_in[...].astype(F32)
@@ -225,7 +223,6 @@
     for k in range(1, groups):
         sum_copy(lax.rem(chip + k, groups), chip, k).wait_send()
     pair.wait_send()
-    keep_out.wait()
     for t in range(supers - 1):
         @pl.when(s > t)
         def _():
@@ -281,13 +278,12 @@
     solved, reply = pl.pallas_call(
         functools.partial(kernel, (supers, ranks, zs, xs)),
         out_shape=(
-            jax.ShapeDtypeStruct((count, width), BF16),
-            jax.ShapeDtypeStruct((rows, width), F32),
+            pltpu.VMEM((count, width), BF16),
+            pltpu.VMEM((rows, width), F32),
         ),
         in_specs=[whole] * 5,
-        out_specs=(whole, vmem),
+        out_specs=(vmem, vmem),
         scratch_shapes=[
-            pltpu.VMEM((count, width), BF16),
             pltpu.VMEM((ranks, columns, width), BF16),
             pltpu.VMEM((count, width), BF16),
             pltpu.VMEM((width, width), F32),
@@ -307,21 +303,24 @@
             pltpu.VMEM((groups, rows, width), F32),
             pltpu.VMEM((groups, rows, width), wire),
             pltpu.VMEM((groups, rows, width), wire),
-            dma((6,)), dma((zs,)), dma((zs, xs)), dma((zs, xs)), dma((ranks,)),
+            dma((5,)), dma((zs,)), dma((zs, xs)), dma((zs, xs)), dma((ranks,)),
             dma((supers,)), dma((supers,)), dma((supers,)), dma((supers,)),
             dma, dma, dma((groups,)), dma((groups,)),
         ],
         compiler_params=pltpu.CompilerParams(
             collective_id=0, has_side_effects=True, vmem_limit_bytes=LIMIT
         ),
-    )(right_sides, stripe.T, inverses, structure, heater_wattages.T)
+    )(*(
+        pltpu.with_memory_space_constraint(value, pltpu.HBM)
+        for value in (right_sides, stripe.T, inverses, structure, heater_wattages.T)
+    ))
     return pl.pallas_call(
         write_out,
         out_shape=(
             jax.ShapeDtypeStruct((count, width), BF16),
             jax.ShapeDtypeStruct((rows, width), F32),
         ),
-        in_specs=[whole, whole],
+        in_specs=[vmem, vmem],
         out_specs=(whole, whole),
         scratch_shapes=[dma((2,))],
     )(solved, reply)

time: 30.1 us -> 28.9 us (0.960)
  Pallas kernels: 29.3 us -> 26.8 us
  local copies, waits for them, and re-layouts: 0 us -> 1.21 us
    pallas_call x1, Pallas kernels: 3.35 us -> 1.44 us  [body(): pl.pallas_call(write_out, out_shape=(jax.ShapeDtypeStruct((count, width),...]
    unnamed x0 -> x4, local copies, waits for them, and re-layouts: none -> 1.21 us
    pallas_call x1, Pallas kernels: 26 us -> 25.4 us  [body(): pl.pallas_call(functools.partial(kernel, (supers, ranks, zs, xs)), out_sh...]
where the time goes in v3:
time: 28.9 us; the launch traced here: 28.7 us
  Pallas kernels  26.8 us (93%)
  local copies, waits for them, and re-layouts  1.21 us (4%)
  between operations  0.65 us (2%)
    pallas_call x1, Pallas kernels, body(): pl.pallas_call(functools.partial(kernel, (supers, ranks, zs, xs)), out_sh...  25.4 us
    pallas_call x1, Pallas kernels, body(): pl.pallas_call(write_out, out_shape=(jax.ShapeDtypeStruct((count, width),...  1.44 us
    unnamed x4, local copies, waits for them, and re-layouts  1.21 us

profile of v3, /device:TPU:0, one launch (start us, length us, event | category | flops | bytes accessed | tf_op | source)
XLA Modules:
  0.0 28.7 jit_solution(3980347849855717679)
XLA Ops:
  0.6 25.4 %shard_map.68 = (bf16[64,384]{1,0:T(8,128)(2,1)S(1)}, f32[16,384]{1,0:T(8,128)S(1)}) custom-call(bf16[64,384]{1,0:T(8,128)(2,1)} %sides_any.1, bf16[48,384]{1,0:T(8,128)(2,1)} %bitcast.2, f32[1,384,384]{2,1,0:T(8,128)} %inverse_any.1, s32[2,2]{1,0:T(2,128)} %structure_any.1, bf16[64,256]{1,0:T(8,128)(2,1)} %bitcast.3), custom_call_target="tpu_custom_call" | custom-call | tf_op jit(solution)/shard_map/pallas_call | solution.py:278
  26.0 0.0 copy-start
  26.0 0.6 %copy-done = bf16[64,384]{1,0:T(8,128)(2,1)} copy-done((bf16[64,384]{1,0:T(8,128)(2,1)}, bf16[64,384]{1,0:T(8,128)(2,1)S(1)}, u32[]{:S(2)}) %copy-start) | copy-done | bytes 49176
  26.6 0.0 copy-start.1
  26.6 0.6 %copy-done.1 = f32[16,384]{1,0:T(8,128)} copy-done((f32[16,384]{1,0:T(8,128)}, f32[16,384]{1,0:T(8,128)S(1)}, u32[]{:S(2)}) %copy-start.1) | copy-done | bytes 24600
  27.2 1.4 %shard_map.69 = (bf16[64,384]{1,0:T(8,128)(2,1)}, f32[16,384]{1,0:T(8,128)}) custom-call(bf16[64,384]{1,0:T(8,128)(2,1)} %copy-done, f32[16,384]{1,0:T(8,128)} %copy-done.1), custom_call_target="tpu_custom_call" | custom-call | tf_op jit(solution)/shard_map/pallas_call | solution.py:317
Async XLA Ops:
  26.0 0.6 %copy-start = (bf16[64,384]{1,0:T(8,128)(2,1)}, bf16[64,384]{1,0:T(8,128)(2,1)S(1)}, u32[]{:S(2)}) copy-start(bf16[64,384]{1,0:T(8,128)(2,1)S(1)} %get-tuple-element.4.solved_ref) | copy-start | bytes 147460
  26.6 0.6 %copy-start.1 = (f32[16,384]{1,0:T(8,128)}, f32[16,384]{1,0:T(8,128)S(1)}, u32[]{:S(2)}) copy-start(f32[16,384]{1,0:T(8,128)S(1)} %get-tuple-element.5.reply_ref) | copy-start | bytes 73732

commit v4 on v3

--- a/solution.py
+++ b/solution.py
@@ -47,6 +47,12 @@
     def needed(b):
         return b < s * per
 
+    barrier = pltpu.get_barrier_semaphore()
+    pl.semaphore_signal(barrier, inc=1, device_id={"rhs": chip * 2 + 1 - core})
+    for k in range(1, supers):
+        pl.semaphore_signal(barrier, inc=1, device_id={"fac": lax.rem(s + k, supers)})
+    for k in range(1, groups):
+        pl.semaphore_signal(barrier, inc=1, device_id={"rhs": lax.rem(chip + k, groups) * 2 + core})
     loads = [
         pltpu.make_async_copy(stripe_any, factor.at[me], load.at[0]),
         pltpu.make_async_copy(inverse_any.at[0], inverse, load.at[1]),
@@ -57,12 +63,6 @@
     for copy in loads:
         copy.start()
 
-    barrier = pltpu.get_barrier_semaphore()
-    pl.semaphore_signal(barrier, inc=1, device_id={"rhs": chip * 2 + 1 - core})
-    for k in range(1, supers):
-        pl.semaphore_signal(barrier, inc=1, device_id={"fac": lax.rem(s + k, supers)})
-    for k in range(1, groups):
-        pl.semaphore_signal(barrier, inc=1, device_id={"rhs": lax.rem(chip + k, groups) * 2 + core})
     loads[0].wait()
     pl.semaphore_wait(barrier, groups + supers - 1)
 
@@ -86,8 +86,10 @@
 
     @pl.when(needed(me))
     def _():
-        for k in range(1, zs):
-            factor_copy(me, z_send.at[k], rank(lax.rem(z + k, zs), x, core)).start()
+        for zz in range(zs - 1, -1, -1):
+            @pl.when(zz != z)
+            def _():
+                factor_copy(me, z_send.at[zz], rank(zz, x, core)).start()
 
     def relay(k):
         b = rank(lax.rem(z + zs - k, zs), x, core)
@@ -234,8 +236,10 @@
 
     @pl.when(needed(me))
     def _():
-        for k in range(1, zs):
-            factor_copy(me, z_send.at[k], me).wait_send()
+        for zz in range(zs):
+            @pl.when(zz != z)
+            def _():
+                factor_copy(me, z_send.at[zz], me).wait_send()
     for k in range(zs):
         own = rank(lax.rem(z + zs - k, zs), x, core)
 
@@ -323,7 +327,10 @@
         in_specs=[vmem, vmem],
         out_specs=(whole, whole),
         scratch_shapes=[dma((2,))],
-    )(solved, reply)
+    )(
+        pltpu.with_memory_space_constraint(solved, pltpu.VMEM),
+        pltpu.with_memory_space_constraint(reply, pltpu.VMEM),
+    )
 
 
 def solution(mesh):

time: 28.9 us -> 26.2 us (0.907)
  Pallas kernels: 26.8 us -> 25.4 us
  local copies, waits for them, and re-layouts: 1.21 us -> 0 us
    unnamed x4 -> x0, local copies, waits for them, and re-layouts: 1.21 us -> none
    pallas_call x1, Pallas kernels: 1.44 us -> 0.64 us  [body(): pl.pallas_call(write_out, out_shape=(jax.ShapeDtypeStruct((count, width),...]
    pallas_call x1, Pallas kernels: 25.4 us -> 24.7 us  [body(): pl.pallas_call(functools.partial(kernel, (supers, ranks, zs, xs)), out_sh...]
where the time goes in v4:
time: 26.2 us; the launch traced here: 26 us
  Pallas kernels  25.4 us (97%)
  between operations  0.64 us (2%)
    pallas_call x1, Pallas kernels, body(): pl.pallas_call(functools.partial(kernel, (supers, ranks, zs, xs)), out_sh...  24.7 us
    pallas_call x1, Pallas kernels, body(): pl.pallas_call(write_out, out_shape=(jax.ShapeDtypeStruct((count, width),...  0.64 us

profile of v4, /device:TPU:0, one launch (start us, length us, event | category | flops | bytes accessed | tf_op | source)
XLA Modules:
  0.0 26.0 jit_solution(14572489138083323822)
XLA Ops:
  0.6 24.7 %shard_map.68 = (bf16[64,384]{1,0:T(8,128)(2,1)S(1)}, f32[16,384]{1,0:T(8,128)S(1)}) custom-call(bf16[64,384]{1,0:T(8,128)(2,1)} %sides_any.1, bf16[48,384]{1,0:T(8,128)(2,1)} %bitcast.2, f32[1,384,384]{2,1,0:T(8,128)} %inverse_any.1, s32[2,2]{1,0:T(2,128)} %structure_any.1, bf16[64,256]{1,0:T(8,128)(2,1)} %bitcast.3), custom_call_target="tpu_custom_call" | custom-call | tf_op jit(solution)/shard_map/pallas_call | solution.py:282
  25.4 0.6 %shard_map.69 = (bf16[64,384]{1,0:T(8,128)(2,1)}, f32[16,384]{1,0:T(8,128)}) custom-call(bf16[64,384]{1,0:T(8,128)(2,1)S(1)} %get-tuple-element.4.solved_ref, f32[16,384]{1,0:T(8,128)S(1)} %get-tuple-element.5.reply_ref), custom_call_target="tpu_custom_call" | custom-call | tf_op jit(solution)/shard_map/pallas_call | solution.py:321

commit v5 on v4

--- a/solution.py
+++ b/solution.py
@@ -26,7 +26,7 @@
 def kernel(
     shape, sides_any, stripe_any, inverse_any, structure_any, watts_any, out_ref, reply_ref,
     factor, sides, inverse, keeps, watts_in, watts, watts_own, plain, turned, base, fwd, fwd_in,
-    upd_out, upd_in, pair_out, pair_in, mine, sum_out, sum_in,
+    upd_out_a, upd_out_b, upd_in_a, upd_in_b, pair_out, pair_in, mine, sum_out, sum_in,
     load, z_send, x_send, c_send, factor_recv, f_send, f_recv, u_send, u_recv,
     pair_send, pair_recv, s_send, s_recv,
 ):
@@ -78,10 +78,13 @@
             recv_sem=f_recv.at[t], device_id={"fac": where},
         )
 
-    def update_copy(t, where):
+    cuts = ((upd_out_a, upd_in_a, 0, 256), (upd_out_b, upd_in_b, 256, width))
+
+    def update_copy(t, where, half):
         return pltpu.make_async_remote_copy(
-            src_ref=upd_out.at[where], dst_ref=upd_in.at[t], send_sem=u_send.at[where],
-            recv_sem=u_recv.at[t], device_id={"fac": where},
+            src_ref=cuts[half][0].at[where], dst_ref=cuts[half][1].at[t],
+            send_sem=u_send.at[where, half], recv_sem=u_recv.at[t, half],
+            device_id={"fac": where},
         )
 
     @pl.when(needed(me))
@@ -109,21 +112,16 @@
     plain[:width] = high
     plain[width:] = low
     turned[:, :width] = high
-    turned[:, width:2 * width] = low
-    turned[:, 2 * width:] = high
+    turned[:, width:] = low
     loads[2].wait()
     loads[4].wait()
 
     def twice(value):
         return jnp.concatenate([value, value], axis=1)
 
-    def thrice(value):
-        a_high, a_low = split(value)
-        return jnp.concatenate([a_high, a_high, a_low], axis=1)
-
     @pl.when(s == 0)
     def _():
-        fwd[...] = mul(twice(sides[...]), turned[:, :2 * width], NT).astype(BF16)
+        fwd[...] = mul(twice(sides[...]), turned[...], NT).astype(BF16)
         for k in range(1, supers):
             forward_copy(0, k, k).start()
 
@@ -164,7 +162,7 @@
                 forward_copy(t, 0, s).wait_recv()
                 keep = keeps[s, t].astype(F32)
                 base[...] -= keep * mul(fwd_in[t], block(t), NN)
-        fwd[...] = mul(thrice(base[...]), turned[...], NT).astype(BF16)
+        fwd[...] = mul(twice(base[...].astype(BF16)), turned[...], NT).astype(BF16)
         for k in range(2, supers):
             @pl.when(s < k)
             def _():
@@ -175,8 +173,9 @@
     for t in range(supers - 1, 0, -1):
         @pl.when(s < t)
         def _():
-            update_copy(t, s).wait_recv()
-            base[...] -= mul(twice(upd_in[t]), plain[...], NN)
+            for half, (_, arrived, first, end) in enumerate(cuts):
+                update_copy(t, s, half).wait_recv()
+                base[...] -= mul(arrived[t], plain[first:end], NN)
             if t - 1 == 0:
                 out_ref[...] = base[...].astype(BF16)
             else:
@@ -187,8 +186,10 @@
         @pl.when(s > t)
         def _():
             keep = keeps[s, t].astype(F32)
-            upd_out[t] = (keep * mul(out_ref[...], block(t), NT)).astype(BF16)
-            update_copy(s, t).start()
+            for half, (leaving, _, first, end) in enumerate(cuts):
+                rows = block(t)[first:end]
+                leaving[t] = (keep * mul(out_ref[...], rows, NT)).astype(BF16)
+                update_copy(s, t, half).start()
 
     def product(first):
         rows = watts_own[first:first + groups]
@@ -213,8 +214,9 @@
             recv_sem=s_recv.at[source], device_id={"rhs": target * 2 + core},
         )
 
+    step = jnp.where(2 * z >= zs, 1, groups - 1)
     for k in range(1, groups):
-        sum_copy(lax.rem(chip + k, groups), chip, k).start()
+        sum_copy(lax.rem(chip + k * step, groups), chip, k).start()
     total = mine[chip]
     for k in range(1, groups):
         source = lax.rem(chip + groups - k, groups)
@@ -223,12 +225,13 @@
     reply_ref[...] = total
 
     for k in range(1, groups):
-        sum_copy(lax.rem(chip + k, groups), chip, k).wait_send()
+        sum_copy(lax.rem(chip + k * step, groups), chip, k).wait_send()
     pair.wait_send()
     for t in range(supers - 1):
         @pl.when(s > t)
         def _():
-            update_copy(s, t).wait_send()
+            for half in range(2):
+                update_copy(s, t, half).wait_send()
     for k in range(1, supers):
         @pl.when(s < k)
         def _():
@@ -296,19 +299,21 @@
             pltpu.VMEM((ranks, rows, count), F32),
             pltpu.VMEM((ranks, rows, count), F32),
             pltpu.VMEM((2 * width, width), BF16),
-            pltpu.VMEM((width, 3 * width), BF16),
+            pltpu.VMEM((width, 2 * width), BF16),
             pltpu.VMEM((count, width), F32),
             pltpu.VMEM((count, width), BF16),
             pltpu.VMEM((supers, count, width), BF16),
-            pltpu.VMEM((supers, count, width), BF16),
-            pltpu.VMEM((supers, count, width), BF16),
+            pltpu.VMEM((supers, count, 256), BF16),
+            pltpu.VMEM((supers, count, width - 256), BF16),
+            pltpu.VMEM((supers, count, 256), BF16),
+            pltpu.VMEM((supers, count, width - 256), BF16),
             pltpu.VMEM((groups, rows, width), wire),
             pltpu.VMEM((groups, rows, width), wire),
             pltpu.VMEM((groups, rows, width), F32),
             pltpu.VMEM((groups, rows, width), wire),
             pltpu.VMEM((groups, rows, width), wire),
             dma((5,)), dma((zs,)), dma((zs, xs)), dma((zs, xs)), dma((ranks,)),
-            dma((supers,)), dma((supers,)), dma((supers,)), dma((supers,)),
+            dma((supers,)), dma((supers,)), dma((supers, 2)), dma((supers, 2)),
             dma, dma, dma((groups,)), dma((groups,)),
         ],
         compiler_params=pltpu.CompilerParams(

time: 26.2 us -> 26.1 us (level)
  no operation moved by 1% of the time
where the time goes in v5:
time: 26.1 us; the launch traced here: 25.9 us
  Pallas kernels  25.3 us (97%)
  between operations  0.64 us (2%)
    pallas_call x1, Pallas kernels, body(): pl.pallas_call(functools.partial(kernel, (supers, ranks, zs, xs)), out_sh...  24.6 us
    pallas_call x1, Pallas kernels, body(): pl.pallas_call(write_out, out_shape=(jax.ShapeDtypeStruct((count, width),...  0.64 us

profile of v5, /device:TPU:0, one launch (start us, length us, event | category | flops | bytes accessed | tf_op | source)
XLA Modules:
  0.0 25.9 jit_solution(5808544983580232636)
XLA Ops:
  0.6 24.6 %shard_map.68 = (bf16[64,384]{1,0:T(8,128)(2,1)S(1)}, f32[16,384]{1,0:T(8,128)S(1)}) custom-call(bf16[64,384]{1,0:T(8,128)(2,1)} %sides_any.1, bf16[48,384]{1,0:T(8,128)(2,1)} %bitcast.2, f32[1,384,384]{2,1,0:T(8,128)} %inverse_any.1, s32[2,2]{1,0:T(2,128)} %structure_any.1, bf16[64,256]{1,0:T(8,128)(2,1)} %bitcast.3), custom_call_target="tpu_custom_call" | custom-call | tf_op jit(solution)/shard_map/pallas_call | solution.py:285
  25.3 0.6 %shard_map.69 = (bf16[64,384]{1,0:T(8,128)(2,1)}, f32[16,384]{1,0:T(8,128)}) custom-call(bf16[64,384]{1,0:T(8,128)(2,1)S(1)} %get-tuple-element.4.solved_ref, f32[16,384]{1,0:T(8,128)S(1)} %get-tuple-element.5.reply_ref), custom_call_target="tpu_custom_call" | custom-call | tf_op jit(solution)/shard_map/pallas_call | solution.py:326

commit v6 on v5

--- a/solution.py
+++ b/solution.py
@@ -27,7 +27,7 @@
     shape, sides_any, stripe_any, inverse_any, structure_any, watts_any, out_ref, reply_ref,
     factor, sides, inverse, keeps, watts_in, watts, watts_own, plain, turned, base, fwd, fwd_in,
     upd_out_a, upd_out_b, upd_in_a, upd_in_b, pair_out, pair_in, mine, sum_out, sum_in,
-    load, z_send, x_send, c_send, factor_recv, f_send, f_recv, u_send, u_recv,
+    load, z_send, z_pass, x_send, c_send, factor_recv, f_send, f_recv, u_send, u_recv,
     pair_send, pair_recv, s_send, s_recv,
 ):
     supers, ranks, zs, xs = shape
@@ -87,20 +87,37 @@
             device_id={"fac": where},
         )
 
+    def direct(zz):
+        far_low = (2 * z >= zs) & (zz == 0)
+        far_high = (2 * z < zs) & (zz == zs - 1)
+        return (zz != z) & ~far_low & ~far_high
+
+    def passed_on(zz):
+        to_high = (z == zs - 2) & (2 * zz < zs)
+        to_low = (z == 1) & (2 * zz >= zs)
+        return to_high | to_low
+
+    end = jnp.where(z == 1, 0, zs - 1)
+
     @pl.when(needed(me))
     def _():
         for zz in range(zs - 1, -1, -1):
-            @pl.when(zz != z)
+            @pl.when(direct(zz))
             def _():
                 factor_copy(me, z_send.at[zz], rank(zz, x, core)).start()
 
     def relay(k):
-        b = rank(lax.rem(z + zs - k, zs), x, core)
+        zz = lax.rem(z + zs - k, zs)
+        b = rank(zz, x, core)
 
         @pl.when(needed(b))
         def _():
             if k > 0:
                 factor_copy(b, z_send.at[0], me).wait_recv()
+
+                @pl.when(passed_on(zz))
+                def _():
+                    factor_copy(b, z_pass.at[k], rank(end, x, core)).start()
             for j in range(1, xs):
                 factor_copy(b, x_send.at[k, j], rank(z, lax.rem(x + j, xs), core)).start()
             factor_copy(b, c_send.at[k, 0], rank(z, x, 1 - core)).start()
@@ -173,9 +190,9 @@
     for t in range(supers - 1, 0, -1):
         @pl.when(s < t)
         def _():
-            for half, (_, arrived, first, end) in enumerate(cuts):
+            for half, (_, arrived, first, last) in enumerate(cuts):
                 update_copy(t, s, half).wait_recv()
-                base[...] -= mul(arrived[t], plain[first:end], NN)
+                base[...] -= mul(arrived[t], plain[first:last], NN)
             if t - 1 == 0:
                 out_ref[...] = base[...].astype(BF16)
             else:
@@ -186,8 +203,8 @@
         @pl.when(s > t)
         def _():
             keep = keeps[s, t].astype(F32)
-            for half, (leaving, _, first, end) in enumerate(cuts):
-                rows = block(t)[first:end]
+            for half, (leaving, _, first, last) in enumerate(cuts):
+                rows = block(t)[first:last]
                 leaving[t] = (keep * mul(out_ref[...], rows, NT)).astype(BF16)
                 update_copy(s, t, half).start()
 
@@ -240,14 +257,19 @@
     @pl.when(needed(me))
     def _():
         for zz in range(zs):
-            @pl.when(zz != z)
+            @pl.when(direct(zz))
             def _():
                 factor_copy(me, z_send.at[zz], me).wait_send()
     for k in range(zs):
-        own = rank(lax.rem(z + zs - k, zs), x, core)
+        zz = lax.rem(z + zs - k, zs)
+        own = rank(zz, x, core)
 
         @pl.when(needed(own))
         def _():
+            if k > 0:
+                @pl.when(passed_on(zz))
+                def _():
+                    factor_copy(own, z_pass.at[k], me).wait_send()
             factor_copy(own, c_send.at[k, 0], me).wait_send()
             for j in range(1, xs):
                 factor_copy(own, x_send.at[k, j], me).wait_send()
@@ -312,7 +334,7 @@
             pltpu.VMEM((groups, rows, width), F32),
             pltpu.VMEM((groups, rows, width), wire),
             pltpu.VMEM((groups, rows, width), wire),
-            dma((5,)), dma((zs,)), dma((zs, xs)), dma((zs, xs)), dma((ranks,)),
+            dma((5,)), dma((zs,)), dma((zs,)), dma((zs, xs)), dma((zs, xs)), dma((ranks,)),
             dma((supers,)), dma((supers,)), dma((supers, 2)), dma((supers, 2)),
             dma, dma, dma((groups,)), dma((groups,)),
         ],

time: 26.1 us -> 28 us (1.073)
  Pallas kernels: 25.3 us -> 27.2 us
    pallas_call x1, Pallas kernels: 24.6 us -> 26.6 us  [body(): pl.pallas_call(functools.partial(kernel, (supers, ranks, zs, xs)), out_sh...]
where the time goes in v6:
time: 28 us; the launch traced here: 27.8 us
  Pallas kernels  27.2 us (97%)
  between operations  0.64 us (2%)
    pallas_call x1, Pallas kernels, body(): pl.pallas_call(functools.partial(kernel, (supers, ranks, zs, xs)), out_sh...  26.6 us
    pallas_call x1, Pallas kernels, body(): pl.pallas_call(write_out, out_shape=(jax.ShapeDtypeStruct((count, width),...  0.64 us

profile of v6, /device:TPU:0, one launch (start us, length us, event | category | flops | bytes accessed | tf_op | source)
XLA Modules:
  0.0 27.8 jit_solution(859978757890115729)
XLA Ops:
  0.6 26.6 %shard_map.68 = (bf16[64,384]{1,0:T(8,128)(2,1)S(1)}, f32[16,384]{1,0:T(8,128)S(1)}) custom-call(bf16[64,384]{1,0:T(8,128)(2,1)} %sides_any.1, bf16[48,384]{1,0:T(8,128)(2,1)} %bitcast.2, f32[1,384,384]{2,1,0:T(8,128)} %inverse_any.1, s32[2,2]{1,0:T(2,128)} %structure_any.1, bf16[64,256]{1,0:T(8,128)(2,1)} %bitcast.3), custom_call_target="tpu_custom_call" | custom-call | tf_op jit(solution)/shard_map/pallas_call | solution.py:307
  27.2 0.6 %shard_map.69 = (bf16[64,384]{1,0:T(8,128)(2,1)}, f32[16,384]{1,0:T(8,128)}) custom-call(bf16[64,384]{1,0:T(8,128)(2,1)S(1)} %get-tuple-element.4.solved_ref, f32[16,384]{1,0:T(8,128)S(1)} %get-tuple-element.5.reply_ref), custom_call_target="tpu_custom_call" | custom-call | tf_op jit(solution)/shard_map/pallas_call | solution.py:348

commit v7 on v5

--- a/solution.py
+++ b/solution.py
@@ -49,6 +49,9 @@
 
     barrier = pltpu.get_barrier_semaphore()
     pl.semaphore_signal(barrier, inc=1, device_id={"rhs": chip * 2 + 1 - core})
+    for j in range(1, xs):
+        beside = rank(z, lax.rem(x + j, xs), 1 - core)
+        pl.semaphore_signal(barrier, inc=1, device_id={"rhs": beside})
     for k in range(1, supers):
         pl.semaphore_signal(barrier, inc=1, device_id={"fac": lax.rem(s + k, supers)})
     for k in range(1, groups):
@@ -64,7 +67,7 @@
         copy.start()
 
     loads[0].wait()
-    pl.semaphore_wait(barrier, groups + supers - 1)
+    pl.semaphore_wait(barrier, groups + supers + xs - 2)
 
     def factor_copy(b, send, where):
         return pltpu.make_async_remote_copy(
@@ -102,7 +105,9 @@
             if k > 0:
                 factor_copy(b, z_send.at[0], me).wait_recv()
             for j in range(1, xs):
-                factor_copy(b, x_send.at[k, j], rank(z, lax.rem(x + j, xs), core)).start()
+                other = lax.rem(x + j, xs)
+                factor_copy(b, x_send.at[k, j], rank(z, other, core)).start()
+                factor_copy(b, c_send.at[k, j], rank(z, other, 1 - core)).start()
             factor_copy(b, c_send.at[k, 0], rank(z, x, 1 - core)).start()
 
     relay(0)
@@ -134,7 +139,6 @@
             @pl.when(needed(b))
             def _():
                 factor_copy(b, z_send.at[0], me).wait_recv()
-                factor_copy(b, c_send.at[k, j], rank(z, x, 1 - core)).start()
 
     loads[3].wait()
     watts[...] = watts_in[...].astype(F32).T.reshape(watts.shape)
@@ -251,12 +255,7 @@
             factor_copy(own, c_send.at[k, 0], me).wait_send()
             for j in range(1, xs):
                 factor_copy(own, x_send.at[k, j], me).wait_send()
-        for j in range(1, xs):
-            b = rank(lax.rem(z + zs - k, zs), lax.rem(x + xs - j, xs), core)
-
-            @pl.when(needed(b))
-            def _():
-                factor_copy(b, c_send.at[k, j], me).wait_send()
+                factor_copy(own, c_send.at[k, j], me).wait_send()
 
 
 def write_out(solved_ref, reply_ref, solved_out, reply_out, sem):

time: 26.1 us -> 25.6 us (0.981)
  Pallas kernels: 25.3 us -> 24.8 us
    pallas_call x1, Pallas kernels: 24.6 us -> 24.1 us  [body(): pl.pallas_call(functools.partial(kernel, (supers, ranks, zs, xs)), out_sh...]
where the time goes in v7:
time: 25.6 us; the launch traced here: 25.4 us
  Pallas kernels  24.8 us (97%)
  between operations  0.64 us (2%)
    pallas_call x1, Pallas kernels, body(): pl.pallas_call(functools.partial(kernel, (supers, ranks, zs, xs)), out_sh...  24.1 us
    pallas_call x1, Pallas kernels, body(): pl.pallas_call(write_out, out_shape=(jax.ShapeDtypeStruct((count, width),...  0.64 us

profile of v7, /device:TPU:0, one launch (start us, length us, event | category | flops | bytes accessed | tf_op | source)
XLA Modules:
  0.0 25.4 jit_solution(7385972531027079864)
XLA Ops:
  0.6 24.1 %shard_map.68 = (bf16[64,384]{1,0:T(8,128)(2,1)S(1)}, f32[16,384]{1,0:T(8,128)S(1)}) custom-call(bf16[64,384]{1,0:T(8,128)(2,1)} %sides_any.1, bf16[48,384]{1,0:T(8,128)(2,1)} %bitcast.2, f32[1,384,384]{2,1,0:T(8,128)} %inverse_any.1, s32[2,2]{1,0:T(2,128)} %structure_any.1, bf16[64,256]{1,0:T(8,128)(2,1)} %bitcast.3), custom_call_target="tpu_custom_call" | custom-call | tf_op jit(solution)/shard_map/pallas_call | solution.py:284
  24.8 0.6 %shard_map.69 = (bf16[64,384]{1,0:T(8,128)(2,1)}, f32[16,384]{1,0:T(8,128)}) custom-call(bf16[64,384]{1,0:T(8,128)(2,1)S(1)} %get-tuple-element.4.solved_ref, f32[16,384]{1,0:T(8,128)S(1)} %get-tuple-element.5.reply_ref), custom_call_target="tpu_custom_call" | custom-call | tf_op jit(solution)/shard_map/pallas_call | solution.py:325

commit v8 on v7

--- a/solution.py
+++ b/solution.py
@@ -110,7 +110,8 @@
                 factor_copy(b, c_send.at[k, j], rank(z, other, 1 - core)).start()
             factor_copy(b, c_send.at[k, 0], rank(z, x, 1 - core)).start()
 
-    relay(0)
+    for k in range(zs):
+        relay(k)
 
     loads[1].wait()
     high, low = split(inverse[...])
@@ -130,8 +131,6 @@
         for k in range(1, supers):
             forward_copy(0, k, k).start()
 
-    for k in range(1, zs):
-        relay(k)
     for k in range(zs):
         for j in range(1, xs):
             b = rank(lax.rem(z + zs - k, zs), lax.rem(x + xs - j, xs), core)

time: 25.6 us -> 25.6 us (level)
  no operation moved by 1% of the time
where the time goes in v8:
time: 25.6 us; the launch traced here: 25.4 us
  Pallas kernels  24.8 us (97%)
  between operations  0.64 us (2%)
    pallas_call x1, Pallas kernels, body(): pl.pallas_call(functools.partial(kernel, (supers, ranks, zs, xs)), out_sh...  24.1 us
    pallas_call x1, Pallas kernels, body(): pl.pallas_call(write_out, out_shape=(jax.ShapeDtypeStruct((count, width),...  0.64 us

profile of v8, /device:TPU:0, one launch (start us, length us, event | category | flops | bytes accessed | tf_op | source)
XLA Modules:
  0.0 25.4 jit_solution(15546117243186525810)
XLA Ops:
  0.6 24.1 %shard_map.68 = (bf16[64,384]{1,0:T(8,128)(2,1)S(1)}, f32[16,384]{1,0:T(8,128)S(1)}) custom-call(bf16[64,384]{1,0:T(8,128)(2,1)} %sides_any.1, bf16[48,384]{1,0:T(8,128)(2,1)} %bitcast.2, f32[1,384,384]{2,1,0:T(8,128)} %inverse_any.1, s32[2,2]{1,0:T(2,128)} %structure_any.1, bf16[64,256]{1,0:T(8,128)(2,1)} %bitcast.3), custom_call_target="tpu_custom_call" | custom-call | tf_op jit(solution)/shard_map/pallas_call | solution.py:283
  24.8 0.6 %shard_map.69 = (bf16[64,384]{1,0:T(8,128)(2,1)}, f32[16,384]{1,0:T(8,128)}) custom-call(bf16[64,384]{1,0:T(8,128)(2,1)S(1)} %get-tuple-element.4.solved_ref, f32[16,384]{1,0:T(8,128)S(1)} %get-tuple-element.5.reply_ref), custom_call_target="tpu_custom_call" | custom-call | tf_op jit(solution)/shard_map/pallas_call | solution.py:324
